TPU v7x, 32 devices: a whole 2x2x4 slice. The times are simulated.
32 devices in a mesh: seg: 8 (over z, core), section: 4 (over y, x).
Axes of the slice: x: 2, y: 2, z: 4, core: 2. Of those that a mesh axis runs over, the one named last changes fastest.
Arguments:
- leaving: bfloat16 [8, 4, 272, 4096], P('seg', 'section'), may hold values from -6 to 6
- w_query: bfloat16 [4, 4096, 2048], P('section'), may hold values from -0.09375 to 0.09375
- w_key: bfloat16 [4, 4096, 2048], P('section', None, 'seg'), may hold values from -0.09375 to 0.09375
- w_value: bfloat16 [4, 4096, 4096], P('section', None, 'seg'), may hold values from -0.09375 to 0.09375
- w_gate: bfloat16 [4, 4096], P('section'), may hold values from -0.09375 to 0.09375
- norm_gain: bfloat16 [4, 4096], P('section'), may hold values from 0.5 to 1.5
- memory_matrix: bfloat16 [4, 4096, 2048], P('section', 'seg'), may hold values from -24 to 24
- key_totals: float32 [4, 2048], P('section'), may hold values from 0.02 to 0.5
- doc_starts: int32 [4, 8], P('section'), may hold values 0 or 1
Outputs:
- updated: bfloat16 [8, 4, 272, 4096], P('seg', 'section')
- matrix_next: bfloat16 [4, 4096, 2048], P('section', 'seg')
- totals_next: float32 [4, 2048], P('section')
All inputs are finite; a program needn't handle non-finite values. No bound on the sum of `doc_starts` on one device may be relied on, other than what follows from the above.
Results may differ from a plain program's by a relative error of at most 0.01.
Values may be sent and summed in bfloat16 or wider, within the bound.
A program may use at most 128 MiB of HBM per device.

v0:
```python
import jax
import jax.numpy as jnp
from jax import lax
from jax.experimental import pallas as pl
from jax.experimental.pallas import tpu as pltpu
from jax.sharding import PartitionSpec as P

MEM = 16


highest = lax.Precision.HIGHEST
epsilon = 1e-05


def shifted(shard, axis, by):
    size = lax.axis_size(axis)
    return lax.ppermute(shard, axis, [(i, (i + by) % size) for i in range(size)])


def feature_map(projected):
    return jax.nn.elu(projected) + 1.0


def contract_last(left_rows, right_rows):
    return lax.dot_general(
        left_rows, right_rows, (((1,), (1,)), ((), ())), preferred_element_type=jnp.float32
    )


def contract_first(left_rows, right_rows):
    return lax.dot_general(
        left_rows,
        right_rows,
        (((0,), (0,)), ((), ())),
        precision=highest,
        preferred_element_type=jnp.float32,
    )


def visibility(starts_row):
    seg_total = starts_row.shape[0]
    positions = jnp.arange(seg_total, dtype=jnp.int32)
    last_start = lax.cummax(jnp.where(starts_row == 1, positions, jnp.int32(-1)), axis=0)
    fresh_flag = (last_start < 0).astype(jnp.float32)
    seen_pairs = (
        (positions[:, None] >= last_start[None, :]) & (positions[:, None] < positions[None, :])
    ).astype(jnp.float32)
    seen_final = (positions >= last_start[seg_total - 1]).astype(jnp.float32)
    return (fresh_flag, seen_pairs, seen_final)


def normalized(rows, gain_row):
    wide = rows.astype(jnp.float32)
    inverse_rms = lax.rsqrt(jnp.mean(wide * wide, axis=-1, keepdims=True) + epsilon)
    return (wide * inverse_rms * gain_row.astype(jnp.float32)).astype(jnp.bfloat16)


def solved(mixing, initial):
    size = mixing.shape[0]
    power = -mixing.T
    writes = initial + jnp.dot(power, initial, precision=highest)
    span = 2
    while span < size // MEM:
        power = jnp.dot(power, power, precision=highest)
        writes = writes + jnp.dot(power, writes, precision=highest)
        span *= 2
    return writes


def rows_by_rows(left, right, precision=None):
    return lax.dot_general(
        left,
        right,
        (((1,), (1,)), ((), ())),
        precision=precision,
        preferred_element_type=jnp.float32,
    )


def phi(v):
    return jnp.where(v > 0, v + 1.0, jnp.exp(jnp.minimum(v, 0.0)))


def chain_kernel(
    leaving, w_query, w_key, w_value, w_gate, gain, matrix, totals_in, starts,
    updated, matrix_out, totals_out,
    mem_rows, rows, normed, wq, wk, wv, slots, memory, keys, writes, queries, base, stage, guests,
    final, matrix_new, sims,
    load_sem, shift_send, shift_recv, slot_send, slot_recv, mem_send, mem_recv, key_send, key_recv,
    write_send, write_recv, query_send, query_recv, base_send, base_recv, store_sem,
):
    seg = lax.axis_index("seg")
    section = lax.axis_index("section")
    sections = lax.axis_size("section")
    z = seg // 2
    core = seg % 2
    pair = z + 1 - 2 * (z % 2)
    inner = (z + 1) // 2 == 1
    outer = (z + 1) // 2 != 1
    middle = jnp.where(inner, 3 - z, 3 - pair)
    far = jnp.where(inner, 3 - pair, 3 - z)
    partner = 2 * z + 1 - core
    pair_seg = 2 * pair + core
    pair_cross = 2 * pair + 1 - core
    across_seg = 2 * (3 - z) + core
    after = (section + 1) % sections
    before = (section + sections - 1) % sections
    row_count = rows.shape[0]
    width = slots.shape[1]
    part = keys.shape[2]
    seg_count = keys.shape[0]
    mem_total = memory.shape[0]
    half = width // 2
    pieces = slot_send.shape[1]
    depth = width // pieces

    def remote(src, dst, send, recv, to_seg, to_section=section):
        return pltpu.make_async_remote_copy(
            src_ref=src, dst_ref=dst, send_sem=send, recv_sem=recv,
            device_id=(to_seg, to_section), device_id_type=pl.DeviceIdType.MESH,
        )

    loads = [
        pltpu.make_async_copy(w_key.at[0], wk, load_sem.at[0]),
        pltpu.make_async_copy(w_value.at[0], wv, load_sem.at[1]),
        pltpu.make_async_copy(matrix.at[0], slots.at[0], load_sem.at[2]),
        pltpu.make_async_copy(w_query.at[0], wq, load_sem.at[3]),
    ]
    for load in loads:
        load.start()

    barrier = pltpu.get_barrier_semaphore()
    for to_seg, to_section in (
        (seg, after), (seg, before), (partner, section), (pair_seg, section), (pair_cross, section)
    ):
        pl.semaphore_signal(
            barrier, inc=1, device_id=(to_seg, to_section), device_id_type=pl.DeviceIdType.MESH
        )

    @pl.when(inner)
    def _():
        pl.semaphore_signal(
            barrier, inc=1, device_id=(across_seg, section), device_id_type=pl.DeviceIdType.MESH
        )
        pl.semaphore_wait(barrier, 6)

    @pl.when(outer)
    def _():
        pl.semaphore_wait(barrier, 5)

    mem_shift = remote(
        leaving.at[0, 0, pl.ds(0, MEM)], mem_rows, shift_send.at[0], shift_recv.at[0], seg, after
    )
    mem_shift.start()
    row_shift = remote(leaving.at[0, 0], rows, shift_send.at[1], shift_recv.at[1], seg, after)
    row_shift.start()

    def slot_copy(kind, piece):
        span = pl.ds(piece * depth, depth)
        source = slots.at[1, span] if kind == 3 else matrix.at[0, span]
        to_seg = pair_seg if kind == 1 else across_seg
        return remote(
            source, slots.at[kind, span], slot_send.at[kind - 1, piece],
            slot_recv.at[kind - 1, piece], to_seg,
        )

    def pump(first, last):
        for number in range(first, last):
            if number < pieces:
                @pl.when(outer)
                def _():
                    slot_copy(1, number).start()

                @pl.when(inner)
                def _():
                    slot_copy(2, number).start()
            else:
                @pl.when(inner)
                def _():
                    slot_copy(1, number - pieces).wait_recv()
                    slot_copy(3, number - pieces).start()

    pump(0, 1)

    same_core = [2 * chip + core for chip in (pair, middle, far)]
    other_core = [2 * chip + 1 - core for chip in (z, pair, middle, far)]

    def gather(view, send, recv):
        def copy(index, number, to_seg):
            return remote(view(index), view(index), send.at[number], recv.at[index], to_seg)

        def begin():
            copy(seg, 0, pair_seg).start()

            @pl.when(inner)
            def _():
                copy(seg, 1, across_seg).start()

            copy(seg, 2, partner).start()

        def relay(k):
            index = same_core[k]
            copy(index, 3 + k, partner).wait_recv()

            @pl.when(inner)
            def _():
                copy(index, 6 + k, across_seg if k == 0 else pair_seg).start()

            copy(index, 3 + k, partner).start()

        def arrive():
            for index in other_core:
                copy(index, 0, partner).wait_recv()

        def finish():
            copy(seg, 0, pair_seg).wait_send()
            copy(seg, 2, partner).wait_send()
            for k, index in enumerate(same_core):
                copy(index, 3 + k, partner).wait_send()

            @pl.when(inner)
            def _():
                copy(seg, 1, across_seg).wait_send()
                for k, index in enumerate(same_core):
                    copy(index, 6 + k, pair_seg).wait_send()

        return begin, relay, arrive, finish

    gain_row = gain[...].astype(jnp.float32)

    def normalize(some):
        wide = some.astype(jnp.float32)
        scale = lax.rsqrt(jnp.mean(wide * wide, axis=-1, keepdims=True) + epsilon)
        return (wide * scale * gain_row).astype(jnp.bfloat16)

    mem_begin, mem_relay, mem_arrive, mem_finish = gather(
        lambda index: memory.at[pl.ds(pl.multiple_of(index * MEM, MEM), MEM)], mem_send, mem_recv
    )
    mem_shift.wait_recv()
    memory[pl.ds(pl.multiple_of(seg * MEM, MEM), MEM), :] = normalize(mem_rows[...])
    mem_begin()
    for k in range(3):
        pump(1 + k, 2 + k)
        mem_relay(k)
    pump(4, 5)
    mem_arrive()

    key_begin, key_relay, key_arrive, key_finish = gather(
        lambda index: keys.at[index], key_send, key_recv
    )
    loads[0].wait()
    keys[seg] = phi(
        jnp.dot(memory[...], wk[...], preferred_element_type=jnp.float32)
    ).astype(jnp.bfloat16)
    key_begin()
    pump(5, 6)
    loads[1].wait()
    values = jnp.dot(memory[...], wv[...], preferred_element_type=jnp.float32)
    gate_logits = jnp.sum(
        memory[...].astype(jnp.float32) * w_gate[...].astype(jnp.float32), axis=-1, keepdims=True
    )
    rates = 1.0 / (1.0 + jnp.exp(-gate_logits))
    for k in range(3):
        key_relay(k)
        pump(6 + k, 7 + k)
    key_arrive()
    pump(9, 12)

    row_shift.wait_recv()

    @pl.loop(0, row_count // 16)
    def _(step):
        some = pl.ds(pl.multiple_of(step * 16, 16), 16)
        normed[some, :] = normalize(rows[some, :])

    loads[3].wait()

    @pl.loop(0, seg_count)
    def _(b):
        cols = pl.ds(pl.multiple_of(b * part, part), part)
        queries[0, :, cols] = phi(
            jnp.dot(normed[...], wq[:, cols], preferred_element_type=jnp.float32)
        ).astype(jnp.bfloat16)

    query_out = remote(
        queries.at[0], queries.at[2], query_send.at[0], query_recv.at[1], pair_seg
    )

    @pl.when(outer)
    def _():
        query_out.start()

    query_swap = remote(
        queries.at[0], queries.at[1], query_send.at[1], query_recv.at[0], partner
    )
    query_swap.start()
    pump(12, 14)

    def last_start(positions):
        last = jnp.full(positions.shape, -1, jnp.int32)
        for j in range(seg_count):
            last = jnp.maximum(last, jnp.where((starts[0, j] == 1) & (positions >= j), j, -1))
        return last

    square = (mem_total, mem_total)
    to_segment = lax.broadcasted_iota(jnp.int32, square, 0) // MEM
    from_segment = lax.broadcasted_iota(jnp.int32, square, 1) // MEM
    seen = ((from_segment >= last_start(to_segment)) & (from_segment < to_segment)).astype(
        jnp.float32
    )
    row_segment = lax.broadcasted_iota(jnp.int32, (mem_total, 1), 0) // MEM
    fresh_rows = (last_start(row_segment) < 0).astype(jnp.float32)
    final_segment = jnp.full((mem_total, 1), seg_count - 1, jnp.int32)
    end_last = last_start(final_segment)
    end_rows = (row_segment >= end_last).astype(jnp.float32)
    fresh_end = (end_last[:1] < 0).astype(jnp.float32)

    loads[2].wait()
    gram = jnp.zeros(square, jnp.float32)
    probed = jnp.zeros((mem_total, width), jnp.float32)
    start_scale = jnp.zeros((mem_total, 1), jnp.float32)
    for b in range(seg_count):
        cols = pl.ds(b * part, part)
        block = keys[b]
        gram += rows_by_rows(block, block)
        probed += rows_by_rows(block, slots[0, :, cols])
        start_scale += jnp.sum(
            block.astype(jnp.float32) * totals_in[:, cols], axis=-1, keepdims=True
        )
    visible = seen * gram
    scales = jnp.maximum(
        fresh_rows * start_scale + jnp.sum(visible, axis=-1, keepdims=True), 1.0
    )
    power = -(rates / scales) * visible
    solved_rows = rates * (values - (fresh_rows / scales) * probed)
    span = 1
    while span < seg_count:
        solved_rows += jnp.dot(
            power, solved_rows, precision=highest, preferred_element_type=jnp.float32
        )
        span *= 2
        if span < seg_count:
            power = jnp.dot(power, power, precision=highest, preferred_element_type=jnp.float32)
    write_begin, write_relay, write_arrive, write_finish = gather(
        lambda index: writes.at[index], write_send, write_recv
    )
    writes[seg] = solved_rows.astype(jnp.bfloat16)
    write_begin()

    pump(14, 2 * pieces)
    key_segment = lax.broadcasted_iota(jnp.int32, (1, mem_total), 1) // MEM
    my_segment = jnp.full((1, mem_total), 0, jnp.int32) + seg
    my_last = last_start(my_segment)
    my_mask = ((key_segment >= my_last) & (key_segment < my_segment)).astype(jnp.float32)
    my_fresh = (my_last[:, :1] < 0).astype(jnp.float32)
    similarity = jnp.zeros((row_count, mem_total), jnp.float32)
    query_scale = jnp.zeros((row_count, 1), jnp.float32)
    for b in range(seg_count):
        cols = pl.ds(b * part, part)
        mine = queries[0, :, cols]
        similarity += rows_by_rows(mine, keys[b])
        query_scale += jnp.sum(
            mine.astype(jnp.float32) * totals_in[:, cols], axis=-1, keepdims=True
        )
    similarity *= my_mask
    inverse = 1.0 / jnp.maximum(
        my_fresh * query_scale + jnp.sum(similarity, axis=-1, keepdims=True), 1.0
    )
    sims[...] = similarity.astype(jnp.bfloat16)
    my_scale = my_fresh * inverse

    write_relay(0)

    ended = (solved_rows * end_rows).T
    for b in range(seg_count):
        cols = pl.ds(b * part, part)
        block = keys[b].astype(jnp.float32)
        matrix_new[:, cols] = (
            fresh_end * slots[0, :, cols].astype(jnp.float32)
            + jnp.dot(ended, block, precision=highest, preferred_element_type=jnp.float32)
        ).astype(jnp.bfloat16)
        totals_out[:, cols] = fresh_end * totals_in[:, cols] + jnp.sum(
            end_rows * block, axis=0, keepdims=True
        )
    matrix_store = pltpu.make_async_copy(matrix_new, matrix_out.at[0], store_sem.at[0])
    matrix_store.start()

    write_relay(1)

    def read(rows_at, slot):
        return rows_by_rows(queries[rows_at], slots[slot]).astype(jnp.bfloat16)

    def read_half(rows_at, h):
        return rows_by_rows(queries[rows_at], slots[3, pl.ds(h * half, half)]).astype(
            jnp.bfloat16
        )

    def partner_copy(slot, column):
        return remote(
            stage.at[slot], base.at[column], base_send.at[slot], base_recv.at[column, 0], partner
        )

    def partner_half(h, column):
        cols = pl.ds(h * half, half)
        return remote(
            stage.at[3, :, cols], base.at[column, :, cols], base_send.at[10 + h],
            base_recv.at[column, h], partner,
        )

    guest_slots = (0, 2)

    def guest_copy(number, which, column):
        return remote(
            guests.at[2 * number + which], base.at[column], base_send.at[4 + 2 * number + which],
            base_recv.at[column, 0], pair_cross if which else pair_seg,
        )

    def guest_half(h, which, column):
        cols = pl.ds(h * half, half)
        return remote(
            guests.at[4 + which, :, cols], base.at[column, :, cols],
            base_send.at[12 + 2 * h + which], base_recv.at[column, h],
            pair_cross if which else pair_seg,
        )

    def far_read(h, column):
        cols = pl.ds(h * half, half)
        for piece in range(h * pieces // 2, (h + 1) * pieces // 2):
            slot_copy(3, piece).wait_recv()
        for which in range(2):
            guests[4 + which, :, cols] = read_half(2 + which, h)
            guest_half(h, which, column).start()
        stage[3, :, cols] = read_half(1, h)
        partner_half(h, column).start()
        base[column, :, cols] = read_half(0, h)

    def chip_read(slot, column):
        stage[slot] = read(1, slot)
        partner_copy(slot, column).start()
        base[column] = read(0, slot)

    def guest_read(number, column):
        for which in range(2):
            guests[2 * number + which] = read(2 + which, guest_slots[number])
            guest_copy(number, which, column).start()

    query_swap.wait_recv()
    chip_read(0, seg)
    write_relay(2)
    guest_swap = remote(
        queries.at[2], queries.at[3], query_send.at[2], query_recv.at[2], partner
    )

    @pl.when(inner)
    def _():
        chip_read(1, same_core[0])
        for piece in range(pieces):
            slot_copy(2, piece).wait_recv()
        chip_read(2, same_core[1])
        query_out.wait_recv()
        guest_swap.start()
        guest_swap.wait_recv()
        guest_read(0, seg)
        guest_read(1, same_core[1])
        far_read(0, same_core[2])
        far_read(1, same_core[2])

    write_arrive()

    def combine(column):
        cols = pl.ds(pl.multiple_of(column * width, width), width)
        low = jnp.dot(sims[...], writes[column], preferred_element_type=jnp.float32)
        final[:, cols] = (
            rows[:, cols].astype(jnp.float32)
            + my_scale * base[column].astype(jnp.float32)
            + inverse * low
        ).astype(jnp.bfloat16)
        return pltpu.make_async_copy(
            final.at[:, cols], updated.at[0, 0, :, cols], store_sem.at[1 + column]
        )

    stores = [combine(seg)]
    stores[0].start()

    def landed(column, halves=False):
        if halves:
            partner_half(0, column).wait_recv()
            partner_half(1, column).wait_recv()
        else:
            partner_copy(0, column).wait_recv()

    landed(partner)
    stores.append(combine(partner))
    stores[-1].start()
    for k in range(3):
        @pl.when(outer)
        def _():
            landed(same_core[k], k == 2)

        stores.append(combine(same_core[k]))
        stores[-1].start()
        landed(other_core[k + 1], k == 2)
        stores.append(combine(other_core[k + 1]))
        stores[-1].start()

    mem_shift.wait_send()
    row_shift.wait_send()
    query_swap.wait_send()
    partner_copy(0, seg).wait_send()

    @pl.when(outer)
    def _():
        for piece in range(pieces):
            slot_copy(1, piece).wait_send()
        query_out.wait_send()

    @pl.when(inner)
    def _():
        for piece in range(pieces):
            slot_copy(2, piece).wait_send()
            slot_copy(3, piece).wait_send()
        guest_swap.wait_send()
        for slot in (1, 2):
            partner_copy(slot, seg).wait_send()
        for which in range(2):
            for number in range(2):
                guest_copy(number, which, seg).wait_send()
            partner_half(which, seg).wait_send()
            for h in range(2):
                guest_half(h, which, seg).wait_send()

    mem_finish()
    key_finish()
    write_finish()
    matrix_store.wait()
    for store in stores:
        store.wait()


def chained(
    leaving, w_query, w_key, w_value, w_gate, norm_gain, memory_matrix, key_totals, doc_starts
):
    seg_count = lax.axis_size("seg")
    rows, features = leaving.shape[2:]
    key_width = w_query.shape[2]
    part = w_key.shape[2]
    width = memory_matrix.shape[1]
    mem_total = seg_count * MEM
    short = jnp.bfloat16
    anywhere = pl.BlockSpec(memory_space=pl.ANY)
    near = pl.BlockSpec(memory_space=pltpu.VMEM)
    dma = pltpu.SemaphoreType.DMA
    updated, matrix_next, totals_next = pl.pallas_call(
        chain_kernel,
        out_shape=(
            jax.ShapeDtypeStruct(leaving.shape, short),
            jax.ShapeDtypeStruct(memory_matrix.shape, short),
            jax.ShapeDtypeStruct(key_totals.shape, jnp.float32),
        ),
        in_specs=[
            anywhere, anywhere, anywhere, anywhere, near, near, anywhere, near,
            pl.BlockSpec(memory_space=pltpu.SMEM),
        ],
        out_specs=(anywhere, anywhere, near),
        scratch_shapes=[
            pltpu.VMEM((MEM, features), short),
            pltpu.VMEM((rows, features), short),
            pltpu.VMEM((rows, features), short),
            pltpu.VMEM((features, key_width), short),
            pltpu.VMEM((features, part), short),
            pltpu.VMEM((features, width), short),
            pltpu.VMEM((4, width, key_width), short),
            pltpu.VMEM((mem_total, features), short),
            pltpu.VMEM((seg_count, mem_total, part), short),
            pltpu.VMEM((seg_count, mem_total, width), short),
            pltpu.VMEM((4, rows, key_width), short),
            pltpu.VMEM((seg_count, rows, width), short),
            pltpu.VMEM((4, rows, width), short),
            pltpu.VMEM((6, rows, width), short),
            pltpu.VMEM((rows, features), short),
            pltpu.VMEM((width, key_width), short),
            pltpu.VMEM((rows, mem_total), short),
            dma((4,)), dma((2,)), dma((2,)), dma((3, 8)), dma((3, 8)),
            dma((9,)), dma((seg_count,)), dma((9,)), dma((seg_count,)),
            dma((9,)), dma((seg_count,)), dma((3,)), dma((3,)),
            dma((16,)), dma((seg_count, 2)), dma((1 + seg_count,)),
        ],
        compiler_params=pltpu.CompilerParams(
            collective_id=0, has_side_effects=True, vmem_limit_bytes=63 * 1024 * 1024
        ),
    )(
        leaving, w_query, w_key, w_value, w_gate, norm_gain, memory_matrix, key_totals, doc_starts
    )
    return (updated, matrix_next, totals_next)


def local(
    leaving, w_query, w_key, w_value, w_gate, norm_gain, memory_matrix, key_totals, doc_starts
):
    seg_count = lax.axis_size("seg")
    my_index = lax.axis_index("seg")
    memory_rows = shifted(leaving[0, 0, :MEM], "section", 1)
    entering = shifted(leaving, "section", 1)[0, 0]
    matrix = memory_matrix[0]
    whole_matrix = lax.all_gather(matrix, "seg", axis=0, tiled=True)
    memory = lax.all_gather(normalized(memory_rows, norm_gain[0]), "seg", axis=0, tiled=True)
    key_part = feature_map(jnp.dot(memory, w_key[0], preferred_element_type=jnp.float32)).astype(
        jnp.bfloat16
    )
    value_part = jnp.dot(memory, w_value[0], preferred_element_type=jnp.float32)
    gate_rates = jax.nn.sigmoid(jnp.dot(memory, w_gate[0], preferred_element_type=jnp.float32))
    key_rows = lax.all_gather(key_part, "seg", axis=1, tiled=True)
    fresh_flag, seen_pairs, seen_final = visibility(doc_starts[0])
    key_wide = key_rows.astype(jnp.float32)
    key_sums = key_wide.reshape(seg_count, MEM, -1).sum(axis=1)
    totals = fresh_flag[:, None] * key_totals[0][None, :] + jnp.dot(
        seen_pairs.T, key_sums, precision=highest
    )
    total_rows = jnp.repeat(totals, MEM, axis=0)
    key_scales = jnp.maximum(jnp.sum(total_rows * key_wide, axis=-1), 1.0)
    key_gram = contract_last(key_rows, key_rows)
    seen_cols = jnp.repeat(jnp.repeat(seen_pairs, MEM, axis=0), MEM, axis=1)
    mixing = seen_cols * key_gram * (gate_rates / key_scales)[None, :]
    fresh_rows = jnp.repeat(fresh_flag, MEM)
    probed_keys = contract_last(key_rows, matrix)
    initial = gate_rates[:, None] * (
        value_part - (fresh_rows / key_scales)[:, None] * probed_keys
    )
    write_cols = solved(mixing, initial)
    writes = lax.all_gather(write_cols.astype(jnp.bfloat16), "seg", axis=1, tiled=True)
    fresh_end = fresh_flag[seg_count - 1]
    end_rows = jnp.repeat(seen_final, MEM)
    matrix_next = (
        fresh_end * matrix.astype(jnp.float32)
        + contract_first(write_cols * end_rows[:, None], key_wide)
    ).astype(jnp.bfloat16)
    totals_next = fresh_end * key_totals[0] + jnp.dot(seen_final, key_sums, precision=highest)
    normed = normalized(entering, norm_gain[0])
    queries = feature_map(jnp.dot(normed, w_query[0], preferred_element_type=jnp.float32)).astype(
        jnp.bfloat16
    )
    my_fresh = fresh_flag[my_index]
    column_mask = jnp.repeat(seen_pairs[:, my_index], MEM)
    my_totals = lax.dynamic_slice_in_dim(totals, my_index, 1, 0)
    denominator = jnp.maximum(jnp.sum(queries.astype(jnp.float32) * my_totals, axis=-1), 1.0)
    similarity = contract_last(queries, key_rows) * column_mask[None, :]
    low_rank = jnp.dot(
        similarity.astype(jnp.bfloat16), writes, preferred_element_type=jnp.float32
    )
    base_read = contract_last(queries, whole_matrix)
    updated = (
        entering.astype(jnp.float32) + (my_fresh * base_read + low_rank) / denominator[:, None]
    ).astype(jnp.bfloat16)
    return (updated[None, None], matrix_next[None], totals_next[None])


def solution(mesh):
    fits = mesh.shape["seg"] == 8 and mesh.shape["section"] > 2
    return jax.shard_map(
        chained if fits else local,
        mesh=mesh,
        in_specs=(
            P("seg", "section", None, None),
            P("section", None, None),
            P("section", None, "seg"),
            P("section", None, "seg"),
            P("section", None),
            P("section", None),
            P("section", "seg", None),
            P("section", None),
            P("section", None),
        ),
        out_specs=(P("seg", "section", None, None), P("section", "seg", None), P("section", None)),
        check_vma=False,
    )
```

profile of v0, /device:TPU:0, one launch (start us, length us, event | category | flops | bytes accessed | tf_op | source)
XLA Modules:
  0.0 163.4 jit_solution(6230608204149053224)
XLA Ops:
  0.6 157.4 %shard_map.112 = (bf16[1,1,272,4096]{3,2,1,0:T(8,128)(2,1)}, bf16[1,512,2048]{2,1,0:T(8,128)(2,1)}, f32[1,2048]{1,0:T(1,128)}) custom-call(bf16[1,1,272,4096]{3,2,1,0:T(8,128)(2,1)} %leaving.1, bf16[1,4096,2048]{2,1,0:T(8,128)(2,1)} %w_query.1, bf16[1,4096,256]{2,1,0:T(8,128)(2,1)} %w_key.1, bf16[1,4096,512]{2,1,0:T(8,128)(2,1)} %w_value.1, ...), custom_call_target="tpu_custom_call" | custom-call | tf_op jit(solution)/shard_map/pallas_call | solution.py:553
  158.0 0.0 copy-start
  158.1 3.4 %copy.15 = bf16[1,1,272,4096]{3,2,1,0:T(8,128)(2,1)} copy(bf16[1,1,272,4096]{3,2,1,0:T(8,128)(2,1)} %get-tuple-element.6) | data formatting | bytes 4456448
  161.4 0.0 copy-done
  161.4 0.0 copy-start.1
  161.4 1.3 copy.16
  162.8 0.0 copy-done.1
  162.8 0.6 copy.17
Async XLA Ops:
  158.0 3.4 %copy-start = (bf16[1,512,2048]{2,1,0:T(8,128)(2,1)S(1)}, bf16[1,512,2048]{2,1,0:T(8,128)(2,1)}, u32[]{:S(2)}) copy-start(bf16[1,512,2048]{2,1,0:T(8,128)(2,1)} %get-tuple-element.7) | copy-start | bytes 6291460
  161.4 1.3 copy-start.1
where the time goes:
time: 164 us; the launch traced here: 163 us
  Pallas kernels  157 us (96%)
  local copies, waits for them, and re-layouts  5.31 us (3%)
    pallas_call x1, Pallas kernels, chained(): pl.pallas_call(chain_kernel, out_shape=(jax.ShapeDtypeStruct(leaving.shap...  157 us
    unnamed x7, local copies, waits for them, and re-layouts  5.31 us

commit v1 on v0

--- a/solution.py
+++ b/solution.py
@@ -152,8 +152,18 @@
         leaving.at[0, 0, pl.ds(0, MEM)], mem_rows, shift_send.at[0], shift_recv.at[0], seg, after
     )
     mem_shift.start()
-    row_shift = remote(leaving.at[0, 0], rows, shift_send.at[1], shift_recv.at[1], seg, after)
-    row_shift.start()
+    cut = (row_count // 2 + 15) // 16 * 16
+    bounds = ((0, cut), (cut, row_count))
+    row_shift = []
+    for n, (low, high) in enumerate(bounds):
+        some = pl.ds(low, high - low)
+        row_shift.append(
+            remote(
+                leaving.at[0, 0, some], rows.at[some], shift_send.at[1 + n],
+                shift_recv.at[1 + n], seg, after,
+            )
+        )
+        row_shift[n].start()
 
     def slot_copy(kind, piece):
         span = pl.ds(piece * depth, depth)
@@ -260,41 +270,53 @@
         memory[...].astype(jnp.float32) * w_gate[...].astype(jnp.float32), axis=-1, keepdims=True
     )
     rates = 1.0 / (1.0 + jnp.exp(-gate_logits))
+    def query_copy(kind, n):
+        low, high = bounds[n]
+        span = pl.ds((2 * row_count if kind == 2 else 0) + low, high - low)
+        landing = pl.ds((1 + kind) * row_count + low, high - low)
+        return remote(
+            queries.at[span], queries.at[landing], query_send.at[kind, n],
+            query_recv.at[kind, n], pair_seg if kind == 1 else partner,
+        )
+
+    def make_queries(n):
+        low, high = bounds[n]
+        row_shift[n].wait_recv()
+
+        @pl.loop(low // 16, high // 16)
+        def _(step):
+            some = pl.ds(pl.multiple_of(step * 16, 16), 16)
+            normed[some, :] = normalize(rows[some, :])
+
+        if n == 0:
+            loads[3].wait()
+
+        @pl.loop(0, seg_count)
+        def _(b):
+            cols = pl.ds(pl.multiple_of(b * part, part), part)
+            queries[low:high, cols] = phi(
+                jnp.dot(normed[low:high, :], wq[:, cols], preferred_element_type=jnp.float32)
+            ).astype(jnp.bfloat16)
+
+        @pl.when(outer)
+        def _():
+            query_copy(1, n).start()
+
+        query_copy(0, n).start()
+
+    def pass_guests(n):
+        @pl.when(inner)
+        def _():
+            query_copy(1, n).wait_recv()
+            query_copy(2, n).start()
+
+    pump(6, 8)
+    make_queries(0)
     for k in range(3):
         key_relay(k)
-        pump(6 + k, 7 + k)
+        pump(8 + k, 9 + k)
     key_arrive()
-    pump(9, 12)
-
-    row_shift.wait_recv()
-
-    @pl.loop(0, row_count // 16)
-    def _(step):
-        some = pl.ds(pl.multiple_of(step * 16, 16), 16)
-        normed[some, :] = normalize(rows[some, :])
-
-    loads[3].wait()
-
-    @pl.loop(0, seg_count)
-    def _(b):
-        cols = pl.ds(pl.multiple_of(b * part, part), part)
-        queries[0, :, cols] = phi(
-            jnp.dot(normed[...], wq[:, cols], preferred_element_type=jnp.float32)
-        ).astype(jnp.bfloat16)
-
-    query_out = remote(
-        queries.at[0], queries.at[2], query_send.at[0], query_recv.at[1], pair_seg
-    )
-
-    @pl.when(outer)
-    def _():
-        query_out.start()
-
-    query_swap = remote(
-        queries.at[0], queries.at[1], query_send.at[1], query_recv.at[0], partner
-    )
-    query_swap.start()
-    pump(12, 14)
+    pump(11, 12)
 
     def last_start(positions):
         last = jnp.full(positions.shape, -1, jnp.int32)
@@ -347,7 +369,11 @@
     writes[seg] = solved_rows.astype(jnp.bfloat16)
     write_begin()
 
+    pump(12, 14)
+    make_queries(1)
     pump(14, 2 * pieces)
+    pass_guests(0)
+
     key_segment = lax.broadcasted_iota(jnp.int32, (1, mem_total), 1) // MEM
     my_segment = jnp.full((1, mem_total), 0, jnp.int32) + seg
     my_last = last_start(my_segment)
@@ -357,7 +383,7 @@
     query_scale = jnp.zeros((row_count, 1), jnp.float32)
     for b in range(seg_count):
         cols = pl.ds(b * part, part)
-        mine = queries[0, :, cols]
+        mine = queries[:row_count, cols]
         similarity += rows_by_rows(mine, keys[b])
         query_scale += jnp.sum(
             mine.astype(jnp.float32) * totals_in[:, cols], axis=-1, keepdims=True
@@ -387,14 +413,6 @@
 
     write_relay(1)
 
-    def read(rows_at, slot):
-        return rows_by_rows(queries[rows_at], slots[slot]).astype(jnp.bfloat16)
-
-    def read_half(rows_at, h):
-        return rows_by_rows(queries[rows_at], slots[3, pl.ds(h * half, half)]).astype(
-            jnp.bfloat16
-        )
-
     def partner_copy(slot, column):
         return remote(
             stage.at[slot], base.at[column], base_send.at[slot], base_recv.at[column, 0], partner
@@ -427,43 +445,48 @@
         cols = pl.ds(h * half, half)
         for piece in range(h * pieces // 2, (h + 1) * pieces // 2):
             slot_copy(3, piece).wait_recv()
+        part_read = rows_by_rows(queries[...], slots[3, pl.ds(h * half, half)]).astype(
+            jnp.bfloat16
+        )
         for which in range(2):
-            guests[4 + which, :, cols] = read_half(2 + which, h)
+            guests[4 + which, :, cols] = part_read[
+                (2 + which) * row_count : (3 + which) * row_count
+            ]
             guest_half(h, which, column).start()
-        stage[3, :, cols] = read_half(1, h)
+        stage[3, :, cols] = part_read[row_count : 2 * row_count]
         partner_half(h, column).start()
-        base[column, :, cols] = read_half(0, h)
+        base[column, :, cols] = part_read[:row_count]
 
     def chip_read(slot, column):
-        stage[slot] = read(1, slot)
+        part_read = rows_by_rows(queries[: 2 * row_count], slots[slot]).astype(jnp.bfloat16)
+        stage[slot] = part_read[row_count:]
         partner_copy(slot, column).start()
-        base[column] = read(0, slot)
+        base[column] = part_read[:row_count]
 
     def guest_read(number, column):
+        part_read = rows_by_rows(
+            queries[2 * row_count :], slots[guest_slots[number]]
+        ).astype(jnp.bfloat16)
         for which in range(2):
-            guests[2 * number + which] = read(2 + which, guest_slots[number])
+            guests[2 * number + which] = part_read[which * row_count : (1 + which) * row_count]
             guest_copy(number, which, column).start()
 
-    query_swap.wait_recv()
+    for n in range(2):
+        query_copy(0, n).wait_recv()
     chip_read(0, seg)
     write_relay(2)
-    guest_swap = remote(
-        queries.at[2], queries.at[3], query_send.at[2], query_recv.at[2], partner
-    )
+    pass_guests(1)
 
     @pl.when(inner)
     def _():
         chip_read(1, same_core[0])
+        for n in range(2):
+            query_copy(2, n).wait_recv()
+        guest_read(0, seg)
         for piece in range(pieces):
             slot_copy(2, piece).wait_recv()
+        guest_read(1, same_core[1])
         chip_read(2, same_core[1])
-        query_out.wait_recv()
-        guest_swap.start()
-        guest_swap.wait_recv()
-        guest_read(0, seg)
-        guest_read(1, same_core[1])
-        far_read(0, same_core[2])
-        far_read(1, same_core[2])
 
     write_arrive()
 
@@ -493,6 +516,12 @@
     stores.append(combine(partner))
     stores[-1].start()
     for k in range(3):
+        if k == 2:
+            @pl.when(inner)
+            def _():
+                far_read(0, same_core[2])
+                far_read(1, same_core[2])
+
         @pl.when(outer)
         def _():
             landed(same_core[k], k == 2)
@@ -504,22 +533,25 @@
         stores[-1].start()
 
     mem_shift.wait_send()
-    row_shift.wait_send()
-    query_swap.wait_send()
+    for n in range(2):
+        row_shift[n].wait_send()
+        query_copy(0, n).wait_send()
     partner_copy(0, seg).wait_send()
 
     @pl.when(outer)
     def _():
         for piece in range(pieces):
             slot_copy(1, piece).wait_send()
-        query_out.wait_send()
+        for n in range(2):
+            query_copy(1, n).wait_send()
 
     @pl.when(inner)
     def _():
         for piece in range(pieces):
             slot_copy(2, piece).wait_send()
             slot_copy(3, piece).wait_send()
-        guest_swap.wait_send()
+        for n in range(2):
+            query_copy(2, n).wait_send()
         for slot in (1, 2):
             partner_copy(slot, seg).wait_send()
         for which in range(2):
@@ -573,16 +605,16 @@
             pltpu.VMEM((mem_total, features), short),
             pltpu.VMEM((seg_count, mem_total, part), short),
             pltpu.VMEM((seg_count, mem_total, width), short),
-            pltpu.VMEM((4, rows, key_width), short),
+            pltpu.VMEM((4 * rows, key_width), short),
             pltpu.VMEM((seg_count, rows, width), short),
             pltpu.VMEM((4, rows, width), short),
             pltpu.VMEM((6, rows, width), short),
             pltpu.VMEM((rows, features), short),
             pltpu.VMEM((width, key_width), short),
             pltpu.VMEM((rows, mem_total), short),
-            dma((4,)), dma((2,)), dma((2,)), dma((3, 8)), dma((3, 8)),
+            dma((4,)), dma((3,)), dma((3,)), dma((3, 8)), dma((3, 8)),
             dma((9,)), dma((seg_count,)), dma((9,)), dma((seg_count,)),
-            dma((9,)), dma((seg_count,)), dma((3,)), dma((3,)),
+            dma((9,)), dma((seg_count,)), dma((3, 2)), dma((3, 2)),
             dma((16,)), dma((seg_count, 2)), dma((1 + seg_count,)),
         ],
         compiler_params=pltpu.CompilerParams(

time: 164 us -> 162 us (0.988)
  Pallas kernels: 157 us -> 155 us
    pallas_call x1, Pallas kernels: 157 us -> 155 us  [chained(): pl.pallas_call(chain_kernel, out_shape=(jax.ShapeDtypeStruct(leaving.shap...]
where the time goes in v1:
time: 162 us; the launch traced here: 161 us
  Pallas kernels  155 us (96%)
  local copies, waits for them, and re-layouts  5.31 us (3%)
    pallas_call x1, Pallas kernels, chained(): pl.pallas_call(chain_kernel, out_shape=(jax.ShapeDtypeStruct(leaving.shap...  155 us
    unnamed x7, local copies, waits for them, and re-layouts  5.31 us

profile of v1, /device:TPU:0, one launch (start us, length us, event | category | flops | bytes accessed | tf_op | source)
XLA Modules:
  0.0 161.4 jit_solution(4897626378042238981)
XLA Ops:
  0.6 155.5 %shard_map.112 = (bf16[1,1,272,4096]{3,2,1,0:T(8,128)(2,1)}, bf16[1,512,2048]{2,1,0:T(8,128)(2,1)}, f32[1,2048]{1,0:T(1,128)}) custom-call(bf16[1,1,272,4096]{3,2,1,0:T(8,128)(2,1)} %leaving.1, bf16[1,4096,2048]{2,1,0:T(8,128)(2,1)} %w_query.1, bf16[1,4096,256]{2,1,0:T(8,128)(2,1)} %w_key.1, bf16[1,4096,512]{2,1,0:T(8,128)(2,1)} %w_value.1, ...), custom_call_target="tpu_custom_call" | custom-call | tf_op jit(solution)/shard_map/pallas_call | solution.py:585
  156.1 0.0 copy-start
  156.1 3.4 %copy.15 = bf16[1,1,272,4096]{3,2,1,0:T(8,128)(2,1)} copy(bf16[1,1,272,4096]{3,2,1,0:T(8,128)(2,1)} %get-tuple-element.6) | data formatting | bytes 4456448
  159.5 0.0 copy-done
  159.5 0.0 copy-start.1
  159.5 1.3 copy.16
  160.8 0.0 copy-done.1
  160.8 0.6 copy.17
Async XLA Ops:
  156.1 3.4 %copy-start = (bf16[1,512,2048]{2,1,0:T(8,128)(2,1)S(1)}, bf16[1,512,2048]{2,1,0:T(8,128)(2,1)}, u32[]{:S(2)}) copy-start(bf16[1,512,2048]{2,1,0:T(8,128)(2,1)} %get-tuple-element.7) | copy-start | bytes 6291460
  159.5 1.3 copy-start.1

commit v2 on v1

--- a/solution.py
+++ b/solution.py
@@ -310,13 +310,11 @@
             query_copy(1, n).wait_recv()
             query_copy(2, n).start()
 
-    pump(6, 8)
-    make_queries(0)
     for k in range(3):
         key_relay(k)
-        pump(8 + k, 9 + k)
+        pump(6 + k, 7 + k)
     key_arrive()
-    pump(11, 12)
+    pump(9, 10)
 
     def last_start(positions):
         last = jnp.full(positions.shape, -1, jnp.int32)
@@ -369,9 +367,13 @@
     writes[seg] = solved_rows.astype(jnp.bfloat16)
     write_begin()
 
-    pump(12, 14)
+    pump(10, 11)
+    make_queries(0)
+    for k in range(3):
+        write_relay(k)
+        pump(11 + k, 12 + k)
+    pump(14, 2 * pieces)
     make_queries(1)
-    pump(14, 2 * pieces)
     pass_guests(0)
 
     key_segment = lax.broadcasted_iota(jnp.int32, (1, mem_total), 1) // MEM
@@ -395,8 +397,6 @@
     sims[...] = similarity.astype(jnp.bfloat16)
     my_scale = my_fresh * inverse
 
-    write_relay(0)
-
     ended = (solved_rows * end_rows).T
     for b in range(seg_count):
         cols = pl.ds(b * part, part)
@@ -411,8 +411,6 @@
     matrix_store = pltpu.make_async_copy(matrix_new, matrix_out.at[0], store_sem.at[0])
     matrix_store.start()
 
-    write_relay(1)
-
     def partner_copy(slot, column):
         return remote(
             stage.at[slot], base.at[column], base_send.at[slot], base_recv.at[column, 0], partner
@@ -474,7 +472,6 @@
     for n in range(2):
         query_copy(0, n).wait_recv()
     chip_read(0, seg)
-    write_relay(2)
     pass_guests(1)
 
     @pl.when(inner)

time: 162 us -> 153 us (0.944)
  Pallas kernels: 155 us -> 147 us
    pallas_call x1, Pallas kernels: 155 us -> 147 us  [chained(): pl.pallas_call(chain_kernel, out_shape=(jax.ShapeDtypeStruct(leaving.shap...]
where the time goes in v2:
time: 153 us
  Pallas kernels  147 us (96%)
  local copies, waits for them, and re-layouts  5.31 us (3%)
    pallas_call x1, Pallas kernels, chained(): pl.pallas_call(chain_kernel, out_shape=(jax.ShapeDtypeStruct(leaving.shap...  147 us
    unnamed x7, local copies, waits for them, and re-layouts  5.31 us

profile of v2, /device:TPU:0, one launch (start us, length us, event | category | flops | bytes accessed | tf_op | source)
XLA Modules:
  0.0 153.0 jit_solution(14495054670717484709)
XLA Ops:
  0.6 147.0 %shard_map.112 = (bf16[1,1,272,4096]{3,2,1,0:T(8,128)(2,1)}, bf16[1,512,2048]{2,1,0:T(8,128)(2,1)}, f32[1,2048]{1,0:T(1,128)}) custom-call(bf16[1,1,272,4096]{3,2,1,0:T(8,128)(2,1)} %leaving.1, bf16[1,4096,2048]{2,1,0:T(8,128)(2,1)} %w_query.1, bf16[1,4096,256]{2,1,0:T(8,128)(2,1)} %w_key.1, bf16[1,4096,512]{2,1,0:T(8,128)(2,1)} %w_value.1, ...), custom_call_target="tpu_custom_call" | custom-call | tf_op jit(solution)/shard_map/pallas_call | solution.py:582
  147.7 0.0 copy-start
  147.7 3.4 %copy.15 = bf16[1,1,272,4096]{3,2,1,0:T(8,128)(2,1)} copy(bf16[1,1,272,4096]{3,2,1,0:T(8,128)(2,1)} %get-tuple-element.6) | data formatting | bytes 4456448
  151.1 0.0 copy-done
  151.1 0.0 copy-start.1
  151.1 1.3 copy.16
  152.4 0.0 copy-done.1
  152.4 0.6 copy.17
Async XLA Ops:
  147.7 3.4 %copy-start = (bf16[1,512,2048]{2,1,0:T(8,128)(2,1)S(1)}, bf16[1,512,2048]{2,1,0:T(8,128)(2,1)}, u32[]{:S(2)}) copy-start(bf16[1,512,2048]{2,1,0:T(8,128)(2,1)} %get-tuple-element.7) | copy-start | bytes 6291460
  151.1 1.3 copy-start.1

commit v3 on v2

--- a/solution.py
+++ b/solution.py
@@ -314,7 +314,7 @@
         key_relay(k)
         pump(6 + k, 7 + k)
     key_arrive()
-    pump(9, 10)
+    pump(9, 11)
 
     def last_start(positions):
         last = jnp.full(positions.shape, -1, jnp.int32)
@@ -367,12 +367,12 @@
     writes[seg] = solved_rows.astype(jnp.bfloat16)
     write_begin()
 
-    pump(10, 11)
+    pump(11, 12)
     make_queries(0)
     for k in range(3):
         write_relay(k)
-        pump(11 + k, 12 + k)
-    pump(14, 2 * pieces)
+        pump(12 + k, 13 + k)
+    pump(15, 2 * pieces)
     make_queries(1)
     pass_guests(0)
 

time: 153 us -> 159 us (1.039)
  Pallas kernels: 147 us -> 153 us
    pallas_call x1, Pallas kernels: 147 us -> 153 us  [chained(): pl.pallas_call(chain_kernel, out_shape=(jax.ShapeDtypeStruct(leaving.shap...]
where the time goes in v3:
time: 159 us
  Pallas kernels  153 us (96%)
  local copies, waits for them, and re-layouts  5.31 us (3%)
    pallas_call x1, Pallas kernels, chained(): pl.pallas_call(chain_kernel, out_shape=(jax.ShapeDtypeStruct(leaving.shap...  153 us
    unnamed x7, local copies, waits for them, and re-layouts  5.31 us

profile of v3, /device:TPU:0, one launch (start us, length us, event | category | flops | bytes accessed | tf_op | source)
XLA Modules:
  0.0 158.6 jit_solution(15412287345759270342)
XLA Ops:
  0.6 152.7 %shard_map.112 = (bf16[1,1,272,4096]{3,2,1,0:T(8,128)(2,1)}, bf16[1,512,2048]{2,1,0:T(8,128)(2,1)}, f32[1,2048]{1,0:T(1,128)}) custom-call(bf16[1,1,272,4096]{3,2,1,0:T(8,128)(2,1)} %leaving.1, bf16[1,4096,2048]{2,1,0:T(8,128)(2,1)} %w_query.1, bf16[1,4096,256]{2,1,0:T(8,128)(2,1)} %w_key.1, bf16[1,4096,512]{2,1,0:T(8,128)(2,1)} %w_value.1, ...), custom_call_target="tpu_custom_call" | custom-call | tf_op jit(solution)/shard_map/pallas_call | solution.py:582
  153.3 0.0 copy-start
  153.3 3.4 %copy.15 = bf16[1,1,272,4096]{3,2,1,0:T(8,128)(2,1)} copy(bf16[1,1,272,4096]{3,2,1,0:T(8,128)(2,1)} %get-tuple-element.6) | data formatting | bytes 4456448
  156.7 0.0 copy-done
  156.7 0.0 copy-start.1
  156.7 1.3 copy.16
  158.0 0.0 copy-done.1
  158.0 0.6 copy.17
Async XLA Ops:
  153.3 3.4 %copy-start = (bf16[1,512,2048]{2,1,0:T(8,128)(2,1)S(1)}, bf16[1,512,2048]{2,1,0:T(8,128)(2,1)}, u32[]{:S(2)}) copy-start(bf16[1,512,2048]{2,1,0:T(8,128)(2,1)} %get-tuple-element.7) | copy-start | bytes 6291460
  156.7 1.3 copy-start.1
